TPU v7x, 512 devices: a whole 4x4x16 slice. The times are simulated.
512 devices in a mesh: grp: 16 (over z_lo, y), dev: 32 (over x, z_hi, core).
Axes of the slice: x: 4, y: 4, z: 16 (z_hi: 4, z_lo: 4; z = z_hi * 4 + z_lo), core: 2. Of those that a mesh axis runs over, the one named last changes fastest.
Arguments:
- spectra: bfloat16 [2, 256, 2048, 384], P(None, None, ('grp', 'dev')), may hold values from -6 to 6
- validity: int32 [2048, 384], P(('grp', 'dev')), may hold values 0 or 1
Outputs:
- correlations: float32 [4, 2048, 128, 128], P(None, ('grp', 'dev'))
All inputs are finite; a program needn't handle non-finite values. No bound on the sum of `validity` on one device may be relied on, other than what follows from the above.
Results may differ from a plain program's by a relative error of at most 0.004.
Values may be sent and summed in bfloat16 or wider, within the bound.
A program may use at most 64 MiB of HBM per device.

v0:
```python
import jax
import jax.numpy as jnp
from jax import lax
from jax.sharding import PartitionSpec as P

LAGS = 128
ROUNDS = 4


def shifted(x, axis, by):
    devices = lax.axis_size(axis)
    return lax.ppermute(x, axis, [(i, (i + by) % devices) for i in range(devices)])


def lag_tables(freqs, lags):
    freq = jnp.arange(freqs, dtype=jnp.int32)[:, None]
    lag = jnp.arange(lags, dtype=jnp.int32)[None, :] - lags // 2
    phase = jnp.mod(freq * lag, 2 * freqs).astype(jnp.float32)
    angle = jnp.pi * phase / freqs
    signed = jnp.stack([jnp.cos(angle), -jnp.sin(angle)], axis=0)
    upper = signed.astype(jnp.bfloat16)
    lower = (signed - upper.astype(jnp.float32)).astype(jnp.bfloat16)
    return jnp.concatenate([upper, lower], axis=2)


def cross_block(own, other):
    real_part = jnp.einsum("fiw,fjw->fij", own[0], other[0], preferred_element_type=jnp.float32)
    real_part = real_part + jnp.einsum(
        "fiw,fjw->fij", own[1], other[1], preferred_element_type=jnp.float32
    )
    imag_part = jnp.einsum("fiw,fjw->fij", own[1], other[0], preferred_element_type=jnp.float32)
    imag_part = imag_part - jnp.einsum(
        "fiw,fjw->fij", own[0], other[1], preferred_element_type=jnp.float32
    )
    return jnp.stack([real_part, imag_part], axis=0).astype(jnp.bfloat16)


def to_lags(returned, split_table, scale):
    lags = split_table.shape[2] // 2
    both = jnp.einsum("pfij,pft->ijt", returned, split_table, preferred_element_type=jnp.float32)
    return (both[:, :, :lags] + both[:, :, lags:]) * scale


def local(spectra, validity):
    windows = spectra.shape[3]
    freqs = spectra.shape[1]
    masked = spectra * validity.astype(jnp.bfloat16)[None, None, :, :]
    regrouped = lax.all_to_all(masked, "dev", split_axis=1, concat_axis=2, tiled=True)
    values = regrouped.astype(jnp.float32)
    power_mean = jnp.sum(values * values, axis=(0, 3)) / windows + 1e-06
    whitened = (values / jnp.sqrt(power_mean)[None, :, :, None]).astype(jnp.bfloat16)
    split_table = lag_tables(freqs, LAGS)
    scale = 1.0 / jnp.sqrt(jnp.float32(windows) * freqs)
    partner = whitened
    outputs = []
    for offset in range(ROUNDS):
        if offset > 0:
            partner = shifted(partner, "grp", 1)
        block_terms = cross_block(whitened, partner)
        returned = lax.all_to_all(block_terms, "dev", split_axis=2, concat_axis=1, tiled=True)
        outputs.append(to_lags(returned, split_table, scale))
    return jnp.stack(outputs, axis=0)


def solution(mesh):
    in_specs = (P(None, None, ("grp", "dev"), None), P(("grp", "dev"), None))
    out_specs = P(None, ("grp", "dev"), None, None)
    return jax.shard_map(local, mesh=mesh, in_specs=in_specs, out_specs=out_specs, check_vma=False)
```

profile of v0, /device:TPU:64, one launch (start us, length us, event | category | flops | bytes accessed | tf_op | source)
XLA Modules:
  0.0 384.4 jit_solution(12298996487330309256)
XLA Ops:
  0.0 0.7 convert_element_type.52
  0.7 2.0 copy_multiply_fusion
  2.7 94.8 %all_to_all.81 = bf16[2,256,4,384]{3,2,0,1:T(4,128)(2,1)S(1)} all-to-all(bf16[2,256,4,384]{3,2,0,1:T(4,128)(2,1)S(1)} %copy_multiply_fusion), channel_id=1, replica_groups=mesh['grp'=16,'dev'=32] {'dev'}, dimensions={1} | all-to-all | bytes 3145728 | tf_op jit(solution)/shard_map/all_to_all | solution.py:48
  97.5 0.9 multiply_reduce_fusion
  98.5 0.3 copy.59
  98.8 0.1 copy.60
  98.8 2.5 copy_bitcast_fusion
  101.3 3.2 reshape.129
  104.5 1.4 divide_convert_fusion
  105.9 1.8 fusion.47
  107.8 3.5 collective-permute-start
  111.3 1.8 fusion.15
  113.1 1.8 fusion.46
  114.9 1.8 fusion.14
  116.8 0.1 pad_maximum_fusion.1
  116.9 1.1 copy.61
  118.0 4.3 %all-to-all-start.1 = ((bf16[2,8,128,128]{3,1,0,2:T(8,128)(2,1)}), bf16[2,8,128,128]{3,1,0,2:T(8,128)(2,1)S(1)}, u32[]{:S(2)}, u32[]{:S(2)}) async-start(bf16[2,8,128,128]{3,1,0,2:T(8,128)(2,1)} %copy.61), calls=%async_computation.1 | async-start | bytes 1048576 | tf_op jit(solution)/shard_map/all_to_all | solution.py:60
  122.3 32.1 %collective-permute-done = bf16[2,8,128,384]{3,2,1,0:T(8,128)(2,1)} collective-permute-done((bf16[2,8,128,384]{3,2,1,0:T(8,128)(2,1)}, bf16[2,8,128,384]{3,2,1,0:T(8,128)(2,1)}, u32[]{:S(2)}, u32[]{:S(2)}) %collective-permute-start) | collective-permute-done | bytes 1572896 | tf_op jit(solution)/shard_map/ppermute | solution.py:12
  154.3 1.9 collective-permute-start.1
  156.2 1.8 fusion.16
  158.1 1.8 fusion.12
  159.9 1.8 fusion.17
  161.7 1.8 fusion.13
  163.6 0.1 pad_maximum_fusion.2
  163.6 1.1 copy.65
  164.8 0.0 all-to-all-done.1
  164.8 17.7 %all-to-all-start.2 = ((bf16[2,8,128,128]{3,1,0,2:T(8,128)(2,1)}), bf16[2,8,128,128]{3,1,0,2:T(8,128)(2,1)S(1)}, u32[]{:S(2)}, u32[]{:S(2)}) async-start(bf16[2,8,128,128]{3,1,0,2:T(8,128)(2,1)} %copy.65), calls=%async_computation.2 | async-start | bytes 1048576 | tf_op jit(solution)/shard_map/all_to_all | solution.py:60
  182.5 26.3 %collective-permute-done.1 = bf16[2,8,128,384]{3,2,1,0:T(8,128)(2,1)S(1)} collective-permute-done((bf16[2,8,128,384]{3,2,1,0:T(8,128)(2,1)}, bf16[2,8,128,384]{3,2,1,0:T(8,128)(2,1)S(1)}, u32[]{:S(2)}, u32[]{:S(2)}) %collective-permute-start.1) | collective-permute-done | bytes 1572896 | tf_op jit(solution)/shard_map/ppermute | solution.py:12
  208.8 1.9 collective-permute-start.2
  210.7 1.6 fusion.18
  212.3 1.6 fusion.10
  213.9 1.6 fusion.19
  215.5 1.6 fusion.11
  217.1 0.1 pad_maximum_fusion.3
  217.2 1.1 copy.69
  218.3 0.0 all-to-all-done.2
  218.3 20.0 %all-to-all-start.3 = ((bf16[2,8,128,128]{3,1,0,2:T(8,128)(2,1)}), bf16[2,8,128,128]{3,1,0,2:T(8,128)(2,1)S(1)}, u32[]{:S(2)}, u32[]{:S(2)}) async-start(bf16[2,8,128,128]{3,1,0,2:T(8,128)(2,1)} %copy.69), calls=%async_computation.3 | async-start | bytes 1048576 | tf_op jit(solution)/shard_map/all_to_all | solution.py:60
  238.3 103.5 %collective-permute-done.2 = bf16[2,8,128,384]{3,2,1,0:T(8,128)(2,1)} collective-permute-done((bf16[2,8,128,384]{3,2,1,0:T(8,128)(2,1)S(1)}, bf16[2,8,128,384]{3,2,1,0:T(8,128)(2,1)}, u32[]{:S(2)}, u32[]{:S(2)}) %collective-permute-start.2) | collective-permute-done | bytes 1572896 | tf_op jit(solution)/shard_map/ppermute | solution.py:12
  341.8 1.8 fusion.20
  343.6 1.8 fusion.8
  345.5 1.8 fusion.21
  347.3 1.8 fusion.9
  349.2 0.1 pad_maximum_fusion.4
  349.2 1.1 copy.73
  350.4 0.0 all-to-all-done.3
  350.4 11.0 %all-to-all-start.4 = ((bf16[2,8,128,128]{3,1,0,2:T(8,128)(2,1)}), bf16[2,8,128,128]{3,1,0,2:T(8,128)(2,1)S(1)}, u32[]{:S(2)}, u32[]{:S(2)}) async-start(bf16[2,8,128,128]{3,1,0,2:T(8,128)(2,1)} %copy.73), calls=%async_computation.4 | async-start | bytes 1048576 | tf_op jit(solution)/shard_map/all_to_all | solution.py:60
  361.4 0.5 fusion.45
  362.0 0.3 convolution_bitcast_fusion.3
  362.4 0.3 convolution_bitcast_fusion.2
  362.8 0.3 convolution_bitcast_fusion.1
  363.2 19.7 %all-to-all-done.4 = bf16[2,8,128,128]{3,1,0,2:T(8,128)(2,1)S(1)} async-done(((bf16[2,8,128,128]{3,1,0,2:T(8,128)(2,1)}), bf16[2,8,128,128]{3,1,0,2:T(8,128)(2,1)S(1)}, u32[]{:S(2)}, u32[]{:S(2)}) %all-to-all-start.4) | async-done | bytes 524320 | tf_op jit(solution)/shard_map/all_to_all | solution.py:60
  382.9 0.3 convolution_bitcast_fusion
  383.3 1.0 pad_maximum_fusion
  (8 shorter events, 0.2 us)
Async XLA Ops:
  107.8 46.5 %collective-permute-start = (bf16[2,8,128,384]{3,2,1,0:T(8,128)(2,1)}, bf16[2,8,128,384]{3,2,1,0:T(8,128)(2,1)}, u32[]{:S(2)}, u32[]{:S(2)}) collective-permute-start(bf16[2,8,128,384]{3,2,1,0:T(8,128)(2,1)} %divide_convert_fusion), channel_id=1, source_target_pairs={{0,32},{32,64},{64,96},{96,128},{128,160},{160,192},{192,224},{224... | collective-permute-start | bytes 4718600 | tf_op jit(solution)/shard_map/ppermute | solution.py:12
  118.0 46.8 %all-to-all-start.1 = ((bf16[2,8,128,128]{3,1,0,2:T(8,128)(2,1)}), bf16[2,8,128,128]{3,1,0,2:T(8,128)(2,1)S(1)}, u32[]{:S(2)}, u32[]{:S(2)}) async-start(bf16[2,8,128,128]{3,1,0,2:T(8,128)(2,1)} %copy.61), calls=%async_computation.1 | async-start | bytes 1048576 | tf_op jit(solution)/shard_map/all_to_all | solution.py:60
  154.3 54.5 %collective-permute-start.1 = (bf16[2,8,128,384]{3,2,1,0:T(8,128)(2,1)}, bf16[2,8,128,384]{3,2,1,0:T(8,128)(2,1)S(1)}, u32[]{:S(2)}, u32[]{:S(2)}) collective-permute-start(bf16[2,8,128,384]{3,2,1,0:T(8,128)(2,1)} %collective-permute-done), channel_id=1, source_target_pairs={{0,32},{32,64},{64,96},{96,128},{128,160},{160,192},{192,224},{224... | collective-permute-start | bytes 4718600 | tf_op jit(solution)/shard_map/ppermute | solution.py:12
  164.8 53.5 %all-to-all-start.2 = ((bf16[2,8,128,128]{3,1,0,2:T(8,128)(2,1)}), bf16[2,8,128,128]{3,1,0,2:T(8,128)(2,1)S(1)}, u32[]{:S(2)}, u32[]{:S(2)}) async-start(bf16[2,8,128,128]{3,1,0,2:T(8,128)(2,1)} %copy.65), calls=%async_computation.2 | async-start | bytes 1048576 | tf_op jit(solution)/shard_map/all_to_all | solution.py:60
  208.8 133.0 %collective-permute-start.2 = (bf16[2,8,128,384]{3,2,1,0:T(8,128)(2,1)S(1)}, bf16[2,8,128,384]{3,2,1,0:T(8,128)(2,1)}, u32[]{:S(2)}, u32[]{:S(2)}) collective-permute-start(bf16[2,8,128,384]{3,2,1,0:T(8,128)(2,1)S(1)} %collective-permute-done.1), channel_id=1, source_target_pairs={{0,32},{32,64},{64,96},{96,128},{128,160},{160,192},{192,224},{224... | collective-permute-start | bytes 4718600 | tf_op jit(solution)/shard_map/ppermute | solution.py:12
  218.3 132.1 %all-to-all-start.3 = ((bf16[2,8,128,128]{3,1,0,2:T(8,128)(2,1)}), bf16[2,8,128,128]{3,1,0,2:T(8,128)(2,1)S(1)}, u32[]{:S(2)}, u32[]{:S(2)}) async-start(bf16[2,8,128,128]{3,1,0,2:T(8,128)(2,1)} %copy.69), calls=%async_computation.3 | async-start | bytes 1048576 | tf_op jit(solution)/shard_map/all_to_all | solution.py:60
  350.4 32.5 %all-to-all-start.4 = ((bf16[2,8,128,128]{3,1,0,2:T(8,128)(2,1)}), bf16[2,8,128,128]{3,1,0,2:T(8,128)(2,1)S(1)}, u32[]{:S(2)}, u32[]{:S(2)}) async-start(bf16[2,8,128,128]{3,1,0,2:T(8,128)(2,1)} %copy.73), calls=%async_computation.4 | async-start | bytes 1048576 | tf_op jit(solution)/shard_map/all_to_all | solution.py:60
where the time goes:
time: 386 us; the launch traced here: 384 us
  waiting for transfers between devices  182 us (47%)
  blocking collectives  94.8 us (25%)
  starting transfers between devices  60.3 us (16%)
  matrix products  29.8 us (8%)
  other arithmetic  9.52 us (2%)
  local copies, waits for them, and re-layouts  8.06 us (2%)
    ppermute x3, waiting for transfers between devices, shifted(): lax.ppermute(x, axis, [(i, (i + by) % devices) for i in range(devices)])  162 us
    all_to_all x1, blocking collectives, local(): lax.all_to_all(masked, 'dev', split_axis=1, concat_axis=2, tiled=True)  94.8 us
    all_to_all x4, starting transfers between devices, local(): lax.all_to_all(block_terms, 'dev', split_axis=2, concat_axis=1, tiled=True)  53 us
    all_to_all x4, waiting for transfers between devices, local(): lax.all_to_all(block_terms, 'dev', split_axis=2, concat_axis=1, tiled=True)  19.7 us
  transfers between devices with their start and end apart: 7, of which 4 were waited for; matrix products, arithmetic and copies ran while one was open for 9% of the time, Pallas kernels for 0%

commit v1 on v0

v1 whole, which is shorter than its diff:
```python
import functools

import jax
import jax.numpy as jnp
import numpy as np
from jax import lax
from jax.experimental import pallas as pl
from jax.experimental.pallas import tpu as pltpu
from jax.sharding import PartitionSpec as P

MESH = pl.DeviceIdType.MESH
FREQS = 256
LAGS = 128
ROUNDS = 4
WINDOWS = 384
GROUP = 128
PEERS = 32
PARTS = 2
SUB = 2
FSUB = FREQS // PEERS // SUB
OWN = GROUP // PEERS
ROWS = OWN * FSUB
LANES = 128


def lag_table():
    freq = np.arange(FREQS, dtype=np.int64)[:, None]
    lag = np.arange(LAGS, dtype=np.int64)[None, :] - LAGS // 2
    angle = np.pi * np.mod(freq * lag, 2 * FREQS) / FREQS
    signed = np.stack([np.cos(angle), -np.sin(angle)], axis=0).astype(np.float32)
    upper = signed.astype(jnp.bfloat16)
    lower = (signed - upper.astype(np.float32)).astype(jnp.bfloat16)
    split = np.stack([upper, lower], axis=0)
    split = split.reshape(2, PARTS, PEERS, SUB, FSUB, LAGS)
    split = split.transpose(3, 2, 1, 4, 0, 5)
    table = np.zeros((SUB, PEERS, 2, PARTS, FSUB, 2, 2, LAGS), dtype=jnp.bfloat16)
    for pair in range(2):
        table[:, :, pair, :, :, :, pair, :] = split
    return table.reshape(SUB, PEERS * 2 * PARTS * FSUB, 4 * LAGS)


def kernel(x_ref, mask_ref, table_ref, out_ref, send, recv, spread, blocks, left, terms, back, home,
           send_sem, recv_sem, ring_send, ring_recv, back_send, back_recv, self_sem):
    grp = lax.axis_index("grp")
    dev = lax.axis_index("dev")
    z_lo, y = grp // 4, grp % 4
    x, z_hi, core = dev // 8, (dev // 2) % 4, dev % 2
    plane = z_hi * 4 + z_lo
    chunk = plane * 2 + core
    alone = x == z_lo

    def worker(q):
        return ((q // 2) % 4 * 4 + y, z_lo * 8 + q // 8 * 2 + q % 2)

    def owner(s):
        return (x * 4 + y, s)

    def ring(by):
        g = (x * 4 + y + by + 16) % 16
        return (z_lo * 4 + g % 4, g // 4 * 8 + z_hi * 2 + core)

    barrier = pltpu.get_barrier_semaphore()

    def greet(i, _):
        @pl.when(jnp.logical_not(jnp.logical_and(alone, i == chunk)))
        def _():
            pl.semaphore_signal(barrier, inc=1, device_id=worker(i), device_id_type=MESH)

        @pl.when(jnp.logical_not(jnp.logical_and(alone, i == dev)))
        def _():
            pl.semaphore_signal(barrier, inc=1, device_id=owner(i), device_id_type=MESH)

        return 0

    lax.fori_loop(0, PEERS, greet, 0)
    for by in (1, -1, 3, -3):
        pl.semaphore_signal(barrier, inc=1, device_id=ring(by), device_id_type=MESH)

    def whiten(k, q):
        masked = x_ref[q * SUB + k].astype(jnp.float32) * mask_ref[...][None]
        power = jnp.sum(jnp.sum(masked * masked, axis=0), axis=1, keepdims=True) / WINDOWS + 1e-06
        send[k, q] = (masked / jnp.sqrt(power)[None]).astype(jnp.bfloat16)

    def in_copy(k, q, s):
        return pltpu.make_async_remote_copy(
            src_ref=send.at[k, q], dst_ref=recv.at[k, s], send_sem=send_sem.at[k, q],
            recv_sem=recv_sem.at[k, s], device_id=worker(q), device_id_type=MESH)

    def in_self(k):
        return pltpu.make_async_copy(send.at[k, chunk], recv.at[k, dev], self_sem.at[k])

    def nth(n):
        step = n // 2
        off = lax.select(step % 2 == 0, 8 - step // 2, step // 2 - 7)
        return (plane + off + 16) % 16 * 2 + (core + n) % 2

    def send_in(k, q):
        here = jnp.logical_and(alone, q == chunk)

        @pl.when(jnp.logical_not(here))
        def _():
            in_copy(k, q, dev).start()

        @pl.when(here)
        def _():
            in_self(k).start()

    def first(n, _):
        whiten(0, nth(n))
        return 0

    lax.fori_loop(0, PEERS, first, 0)
    total = 2 * PEERS + 4 - 2 * alone.astype(jnp.int32)
    pl.semaphore_wait(barrier, total)

    def first_send(n, _):
        send_in(0, nth(n))
        return 0

    lax.fori_loop(0, PEERS, first_send, 0)

    def second(n, _):
        whiten(1, nth(n))
        send_in(1, nth(n))
        return 0

    lax.fori_loop(0, PEERS, second, 0)

    def wait_in(k):
        def body(s, _):
            here = jnp.logical_and(alone, s == dev)

            @pl.when(jnp.logical_not(here))
            def _():
                in_copy(k, s, s).wait_recv()

            @pl.when(here)
            def _():
                in_self(k).wait()

            return 0

        lax.fori_loop(0, PEERS, body, 0)

    def regroup(k):
        for part in range(PARTS):
            for w in range(WINDOWS // LANES):
                spread[w] = recv[k, :, part, :, w * LANES:(w + 1) * LANES].astype(jnp.float32).reshape(
                    PEERS * ROWS, LANES)
            for f in range(FSUB):
                for w in range(WINDOWS // LANES):
                    at = part * WINDOWS + w * LANES
                    blocks[k, 0, f, :, at:at + LANES] = spread[
                        w, pl.ds(f, GROUP, stride=FSUB), :].astype(jnp.bfloat16)

    half = FSUB // 2

    def ring_copy(k, which):
        by, src, dst = (
            (1, blocks.at[k, 0], blocks.at[k, 1]),
            (3, blocks.at[k, 0], blocks.at[k, 3]),
            (1, blocks.at[k, 1, 0:half], blocks.at[k, 2, 0:half]),
            (-1, blocks.at[k, 3, half:FSUB], blocks.at[k, 2, half:FSUB]),
        )[which]
        return pltpu.make_async_remote_copy(
            src_ref=src, dst_ref=dst, send_sem=ring_send.at[k, which], recv_sem=ring_recv.at[k, which],
            device_id=ring(by), device_id_type=MESH)

    def exchange(k):
        wait_in(k)
        regroup(k)
        ring_copy(k, 0).start()
        ring_copy(k, 1).start()

    def cross(k):
        def body(f, _):
            own = blocks[k, 0, f]
            first_part, second_part = own[:, :WINDOWS], own[:, WINDOWS:]
            left[0:GROUP, :] = own
            left[GROUP:, 0:WINDOWS] = second_part
            left[GROUP:, WINDOWS:] = -first_part
            for r in range(ROUNDS):
                product = lax.dot_general(
                    left[...], blocks[k, r, f], (((1,), (1,)), ((), ())), preferred_element_type=jnp.float32)
                for part in range(PARTS):
                    terms[r, pl.ds(part * FSUB + f, GROUP, stride=PARTS * FSUB), :] = product[
                        part * GROUP:(part + 1) * GROUP]
            return 0

        lax.fori_loop(0, FSUB, body, 0)
        for r in range(ROUNDS):
            back[k, :, r] = terms[r].astype(jnp.bfloat16).reshape(PEERS, OWN * PARTS * FSUB, LANES)

    def out_copy(k, s, q):
        return pltpu.make_async_remote_copy(
            src_ref=back.at[k, s], dst_ref=home.at[k, q], send_sem=back_send.at[k, s],
            recv_sem=back_recv.at[k, q], device_id=owner(s), device_id_type=MESH)

    def out_self(k):
        return pltpu.make_async_copy(back.at[k, dev], home.at[k, chunk], self_sem.at[SUB + k])

    def send_out(k):
        def body(n, _):
            step = n // 8
            s = (n // 2) % 4 * 8 + (z_hi + 2 + 2 * (step % 2) + step // 2) % 4 * 2 + (core + n) % 2
            here = jnp.logical_and(alone, s == dev)

            @pl.when(jnp.logical_not(here))
            def _():
                out_copy(k, s, chunk).start()

            @pl.when(here)
            def _():
                out_self(k).start()

            return 0

        lax.fori_loop(0, PEERS, body, 0)

    def forward(k):
        ring_copy(k, 0).wait_recv()
        ring_copy(k, 2).start()
        ring_copy(k, 1).wait_recv()
        ring_copy(k, 3).start()
        ring_copy(k, 2).wait_recv()
        ring_copy(k, 3).wait_recv()

    def wait_out(k):
        def body(q, _):
            here = jnp.logical_and(alone, q == chunk)

            @pl.when(jnp.logical_not(here))
            def _():
                out_copy(k, q, q).wait_recv()

            @pl.when(here)
            def _():
                out_self(k).wait()

            return 0

        lax.fori_loop(0, PEERS, body, 0)

    scale = 1.0 / np.sqrt(np.float32(WINDOWS) * FREQS)

    def to_lags(k):
        def body(n, _):
            r, pair = n // 2, n % 2
            rows = pl.multiple_of(pair * 16, 16)
            values = home[k, :, r, pl.ds(rows, 16), :].reshape(PEERS * 16, LANES)
            both = lax.dot_general(
                values, table_ref[k], (((0,), (0,)), ((), ())), preferred_element_type=jnp.float32)
            lagged = (both[:, :2 * LAGS] + both[:, 2 * LAGS:]) * scale
            for c in range(2):
                piece = lagged[:, c * LAGS:(c + 1) * LAGS]
                if k == 0:
                    out_ref[r, pair * 2 + c] = piece
                else:
                    out_ref[r, pair * 2 + c] += piece
            return 0

        lax.fori_loop(0, ROUNDS * 2, body, 0)

    for k in range(SUB):
        exchange(k)
        forward(k)
        cross(k)
        send_out(k)
    for k in range(SUB):
        wait_out(k)
        to_lags(k)

    for k in range(SUB):
        for which in range(4):
            ring_copy(k, which).wait_send()

        def finish(n, _):
            @pl.when(jnp.logical_not(jnp.logical_and(alone, n == chunk)))
            def _():
                in_copy(k, n, dev).wait_send()

            @pl.when(jnp.logical_not(jnp.logical_and(alone, n == dev)))
            def _():
                out_copy(k, n, chunk).wait_send()

            return 0

        lax.fori_loop(0, PEERS, finish, 0)


def local(spectra, validity):
    pieces = spectra.reshape(PARTS, PEERS * SUB, FSUB, OWN, WINDOWS).transpose(1, 0, 3, 2, 4)
    pieces = pieces.reshape(PEERS * SUB, PARTS, ROWS, WINDOWS)
    mask = jnp.repeat(validity.astype(jnp.float32), FSUB, axis=0)
    table = jnp.asarray(lag_table())
    vmem = pl.BlockSpec(memory_space=pltpu.VMEM)
    dma = pltpu.SemaphoreType.DMA
    return pl.pallas_call(
        kernel,
        out_shape=jax.ShapeDtypeStruct((ROUNDS, OWN, GROUP, LAGS), jnp.float32),
        in_specs=[vmem, vmem, vmem],
        out_specs=vmem,
        scratch_shapes=[
            pltpu.VMEM((SUB, PEERS, PARTS, ROWS, WINDOWS), jnp.bfloat16),
            pltpu.VMEM((SUB, PEERS, PARTS, ROWS, WINDOWS), jnp.bfloat16),
            pltpu.VMEM((WINDOWS // LANES, PEERS * ROWS, LANES), jnp.float32),
            pltpu.VMEM((SUB, ROUNDS, FSUB, GROUP, PARTS * WINDOWS), jnp.bfloat16),
            pltpu.VMEM((2 * GROUP, PARTS * WINDOWS), jnp.bfloat16),
            pltpu.VMEM((ROUNDS, GROUP * PARTS * FSUB, LANES), jnp.float32),
            pltpu.VMEM((SUB, PEERS, ROUNDS, OWN * PARTS * FSUB, LANES), jnp.bfloat16),
            pltpu.VMEM((SUB, PEERS, ROUNDS, OWN * PARTS * FSUB, LANES), jnp.bfloat16),
            dma((SUB, PEERS)), dma((SUB, PEERS)),
            dma((SUB, 4)), dma((SUB, 4)),
            dma((SUB, PEERS)), dma((SUB, PEERS)),
            dma((2 * SUB,)),
        ],
        compiler_params=pltpu.CompilerParams(
            collective_id=1, has_side_effects=True, vmem_limit_bytes=48 << 20),
        name="correlate",
    )(pieces, mask, table)


def solution(mesh):
    in_specs = (P(None, None, ("grp", "dev"), None), P(("grp", "dev"), None))
    out_specs = P(None, ("grp", "dev"), None, None)
    return jax.shard_map(local, mesh=mesh, in_specs=in_specs, out_specs=out_specs, check_vma=False)
```

time: 386 us -> 272 us (0.70)
  the two profiles are of different devices: /device:TPU:64 before, /device:TPU:47 now
where the time goes in v1:
time: 272 us
  Pallas kernels  265 us (97%)
  local copies, waits for them, and re-layouts  7.02 us (3%)
    pallas_call x1, Pallas kernels, local(): pl.pallas_call(kernel, out_shape=jax.ShapeDtypeStruct((ROUNDS, OWN, GROUP...  265 us

profile of v1, /device:TPU:47, one launch (start us, length us, event | category | flops | bytes accessed | tf_op | source)
XLA Modules:
  0.0 271.7 jit_solution(10703004666550750249)
XLA Ops:
  0.0 3.2 %copy.6 = bf16[2,64,4,4,384]{4,2,3,0,1:T(4,128)(2,1)} copy(bf16[2,64,4,4,384]{4,3,2,1,0:T(4,128)(2,1)} %bitcast.5) | data formatting | bytes 3145728 | tf_op jit(solution)/shard_map/reshape | solution.py:292
  3.2 0.0 copy-start.1
  3.2 0.0 copy-start
  3.2 2.8 %reshape.10.x_ref = bf16[64,2,16,384]{3,2,1,0:T(8,128)(2,1)S(1)} reshape(bf16[64,2,4,4,384]{4,3,2,1,0:T(4,128)(2,1)} %bitcast.4) | data formatting | bytes 3145728 | tf_op jit(solution)/shard_map/reshape | solution.py:293
  6.0 0.0 copy-done.1
  6.1 0.0 copy-done
  6.1 264.6 %correlate.1 = f32[4,4,128,128]{3,2,1,0:T(8,128)S(1)} custom-call(bf16[64,2,16,384]{3,2,1,0:T(8,128)(2,1)S(1)} %reshape.10.x_ref, f32[16,384]{1,0:T(8,128)S(1)} %reshape.11.mask_ref, bf16[2,512,512]{2,1,0:T(8,128)(2,1)S(1)} %copy-done), custom_call_target="tpu_custom_call" | custom-call | tf_op jit(solution)/shard_map/correlate/pallas_call | solution.py:298
  270.7 1.0 copy.8
  (3 shorter events, 0.0 us)
Async XLA Ops:
  3.2 2.8 %copy-start.1 = (s32[4,384]{1,0:T(4,128)S(1)}, s32[4,384]{1,0:T(4,128)}, u32[]{:S(2)}) copy-start(s32[4,384]{1,0:T(4,128)} %param.4) | copy-start | bytes 18436
  3.2 2.9 %copy-start = (bf16[2,512,512]{2,1,0:T(8,128)(2,1)S(1)}, bf16[2,512,512]{2,1,0:T(8,128)(2,1)}, u32[]{:S(2)}) copy-start(bf16[2,512,512]{2,1,0:T(8,128)(2,1)} %constant.2.clone.table_ref) | copy-start | bytes 3145732

commit v2 on v1

v2 whole, which is shorter than its diff:
```python
import jax
import jax.numpy as jnp
import numpy as np
from jax import lax
from jax.experimental import pallas as pl
from jax.experimental.pallas import tpu as pltpu
from jax.sharding import PartitionSpec as P

MESH = pl.DeviceIdType.MESH
FREQS = 256
LAGS = 128
ROUNDS = 4
WINDOWS = 384
GROUP = 128
PEERS = 32
PARTS = 2
SUB = 2
FSUB = FREQS // PEERS // SUB
OWN = GROUP // PEERS
ROWS = OWN * FSUB
BACK_ROWS = OWN * PARTS * FSUB
LANES = 128
BATCH = 4


def lag_table():
    freq = np.arange(FREQS, dtype=np.int64)[:, None]
    lag = np.arange(LAGS, dtype=np.int64)[None, :] - LAGS // 2
    angle = np.pi * np.mod(freq * lag, 2 * FREQS) / FREQS
    signed = np.stack([np.cos(angle), -np.sin(angle)], axis=0).astype(np.float32)
    upper = signed.astype(jnp.bfloat16)
    lower = (signed - upper.astype(np.float32)).astype(jnp.bfloat16)
    split = np.stack([upper, lower], axis=0)
    split = split.reshape(2, PARTS, PEERS, SUB, FSUB, LAGS)
    split = split.transpose(3, 2, 1, 4, 0, 5)
    table = np.zeros((SUB, PEERS, 2, PARTS, FSUB, 2, 2, LAGS), dtype=jnp.bfloat16)
    for pair in range(2):
        table[:, :, pair, :, :, :, pair, :] = split
    return table.reshape(SUB, PEERS * 2 * PARTS * FSUB, 4 * LAGS)


def kernel(x_ref, mask_ref, table_ref, out_ref, send, recv, spread, blocks, carry, left, terms, loan, back, home,
           send_sem, recv_sem, ring_send, ring_recv, back_send, back_recv, self_sem):
    grp = lax.axis_index("grp")
    dev = lax.axis_index("dev")
    z_lo, y = grp // 4, grp % 4
    x, z_hi, core = dev // 8, (dev // 2) % 4, dev % 2
    plane = z_hi * 4 + z_lo
    chunk = plane * 2 + core
    flip = 1 - 2 * (z_lo % 2)
    held = (z_lo + flip * x + 4) % 4
    alone = x == 0

    def worker(q):
        at = q // 2
        column = ((z_lo - at) * (1 - 2 * (at % 2)) + 32) % 4
        return (at % 4 * 4 + y, column * 8 + at // 4 * 2 + q % 2)

    def owner(s):
        return (held * 4 + y, s)

    def ring(by):
        g = (held * 4 + y + by + 16) % 16
        column = ((g // 4 - z_lo) * flip + 8) % 4
        return (z_lo * 4 + g % 4, column * 8 + z_hi * 2 + core)

    barrier = pltpu.get_barrier_semaphore()

    def greet(i, _):
        @pl.when(jnp.logical_not(jnp.logical_and(alone, i == chunk)))
        def _():
            pl.semaphore_signal(barrier, inc=1, device_id=worker(i), device_id_type=MESH)

        @pl.when(jnp.logical_not(jnp.logical_and(alone, i == dev)))
        def _():
            pl.semaphore_signal(barrier, inc=1, device_id=owner(i), device_id_type=MESH)

        return 0

    lax.fori_loop(0, PEERS, greet, 0)
    for by in (1, -1, 3, -3, 4, -4):
        pl.semaphore_signal(barrier, inc=1, device_id=ring(by), device_id_type=MESH)

    def whiten(k):
        def body(n, _):
            at = pl.multiple_of(n * BATCH, BATCH)
            masked = x_ref[k, pl.ds(at, BATCH)].astype(jnp.float32) * mask_ref[...][None, None]
            power = jnp.sum(jnp.sum(masked * masked, axis=1, keepdims=True), axis=3, keepdims=True) / WINDOWS + 1e-06
            send[k, pl.ds(at, BATCH)] = (masked / jnp.sqrt(power)).astype(jnp.bfloat16)
            return 0

        lax.fori_loop(0, PEERS // BATCH, body, 0)

    def in_copy(k, q, s):
        return pltpu.make_async_remote_copy(
            src_ref=send.at[k, q], dst_ref=recv.at[k, s], send_sem=send_sem.at[k, q],
            recv_sem=recv_sem.at[k, s], device_id=worker(q), device_id_type=MESH)

    def in_self(k):
        return pltpu.make_async_copy(send.at[k, chunk], recv.at[k, dev], self_sem.at[k])

    def nth(n):
        step = n // 2
        off = lax.select(step % 2 == 0, 8 - step // 2, step // 2 - 7)
        return (plane + off + 16) % 16 * 2 + (core + n) % 2

    def send_in(k):
        def body(n, _):
            q = nth(n)
            here = jnp.logical_and(alone, q == chunk)

            @pl.when(jnp.logical_not(here))
            def _():
                in_copy(k, q, dev).start()

            @pl.when(here)
            def _():
                in_self(k).start()

            return 0

        lax.fori_loop(0, PEERS, body, 0)

    def wait_in(k):
        def body(s, _):
            here = jnp.logical_and(alone, s == dev)

            @pl.when(jnp.logical_not(here))
            def _():
                in_copy(k, s, s).wait_recv()

            @pl.when(here)
            def _():
                in_self(k).wait()

            return 0

        lax.fori_loop(0, PEERS, body, 0)

    def regroup(k):
        for part in range(PARTS):
            for w in range(WINDOWS // LANES):
                spread[w] = recv[k, :, part, :, w * LANES:(w + 1) * LANES].astype(jnp.float32).reshape(
                    PEERS * ROWS, LANES)
            for f in range(FSUB):
                for w in range(WINDOWS // LANES):
                    at = part * WINDOWS + w * LANES
                    blocks[k, 0, f, :, at:at + LANES] = spread[
                        w, pl.ds(f, GROUP, stride=FSUB), :].astype(jnp.bfloat16)

    def ring_copy(by, src, dst, k, which, f):
        return pltpu.make_async_remote_copy(
            src_ref=src, dst_ref=dst, send_sem=ring_send.at[k, which, f], recv_sem=ring_recv.at[k, which, f],
            device_id=ring(by), device_id_type=MESH)

    def next_copy(k, f):
        return ring_copy(1, blocks.at[k, 0, f], blocks.at[k, 1, f], k, 0, f)

    def third_copy(k, f):
        return ring_copy(3, blocks.at[k, 0, f], blocks.at[k, 2, f], k, 1, f)

    def turn_copy(k, f):
        return ring_copy(-3, blocks.at[k, 0, f], carry.at[k, f], k, 2, f)

    def pass_copy(k, f):
        return ring_copy(4, carry.at[k, f], blocks.at[k, 1, f], k, 0, f)

    def loan_copy(k):
        return ring_copy(-1, loan.at[k], back.at[k, 3], k, 3, 0)

    def send_ring(k):
        for f in range(FSUB):
            @pl.when(y < 3)
            def _():
                next_copy(k, f).start()

            @pl.when(y == 3)
            def _():
                turn_copy(k, f).start()

            third_copy(k, f).start()

    def pass_on(k, f):
        @pl.when(y == 0)
        def _():
            turn_copy(k, f).wait_recv()
            pass_copy(k, f).start()

    def end_ring(k):
        for f in range(FSUB):
            @pl.when(y < 3)
            def _():
                next_copy(k, f).wait_send()

            @pl.when(y == 3)
            def _():
                turn_copy(k, f).wait_send()

            @pl.when(y == 0)
            def _():
                pass_copy(k, f).wait_send()

            third_copy(k, f).wait_send()
        loan_copy(k).wait_send()

    def cross(k, one, other, put, ready):
        def body(f, _):
            ready(f)
            own = blocks[k, one, f]
            left[0:GROUP, :] = own
            left[GROUP:, 0:WINDOWS] = own[:, WINDOWS:]
            left[GROUP:, WINDOWS:] = -own[:, :WINDOWS]
            product = lax.dot_general(
                left[...], blocks[k, other, f], (((1,), (1,)), ((), ())), preferred_element_type=jnp.float32)
            for part in range(PARTS):
                terms[pl.ds(part * FSUB + f, GROUP, stride=PARTS * FSUB), :] = product[
                    part * GROUP:(part + 1) * GROUP]
            return 0

        lax.fori_loop(0, FSUB, body, 0)
        put[...] = terms[...].astype(jnp.bfloat16).reshape(PEERS, BACK_ROWS, LANES)

    def out_refs(k, late, s, q):
        if late:
            return back.at[k, 1:ROUNDS, s], home.at[k, q, 1:ROUNDS]
        return back.at[k, 0, s], home.at[k, q, 0]

    def out_copy(k, late, s, q):
        src, dst = out_refs(k, late, s, q)
        return pltpu.make_async_remote_copy(
            src_ref=src, dst_ref=dst, send_sem=back_send.at[k, late, s],
            recv_sem=back_recv.at[k, late, q], device_id=owner(s), device_id_type=MESH)

    def out_self(k, late):
        src, dst = out_refs(k, late, dev, chunk)
        return pltpu.make_async_copy(src, dst, self_sem.at[SUB + 2 * k + late])

    def send_out(k, late):
        def body(n, _):
            s = (x + n // 4) % 4 * 8 + (z_hi + 2 + n) % 4 * 2 + (core + n // 16) % 2
            here = jnp.logical_and(alone, s == dev)

            @pl.when(jnp.logical_not(here))
            def _():
                out_copy(k, late, s, chunk).start()

            @pl.when(here)
            def _():
                out_self(k, late).start()

            return 0

        lax.fori_loop(0, PEERS, body, 0)

    def wait_out(k):
        def body(q, _):
            here = jnp.logical_and(alone, q == chunk)

            @pl.when(jnp.logical_not(here))
            def _():
                for late in range(2):
                    out_copy(k, late, q, q).wait_recv()

            @pl.when(here)
            def _():
                for late in range(2):
                    out_self(k, late).wait()

            return 0

        lax.fori_loop(0, PEERS, body, 0)

    scale = 1.0 / np.sqrt(np.float32(WINDOWS) * FREQS)

    def to_lags(k):
        def body(n, _):
            slot, pair = n // 2, n % 2
            r = slot + (slot == 2).astype(jnp.int32) - (slot == 3).astype(jnp.int32)
            rows = pl.multiple_of(pair * 16, 16)
            values = home[k, :, slot, pl.ds(rows, 16), :].reshape(PEERS * 16, LANES)
            both = lax.dot_general(
                values, table_ref[k], (((0,), (0,)), ((), ())), preferred_element_type=jnp.float32)
            lagged = (both[:, :2 * LAGS] + both[:, 2 * LAGS:]) * scale
            for c in range(2):
                piece = lagged[:, c * LAGS:(c + 1) * LAGS]
                if k == 0:
                    out_ref[r, pair * 2 + c] = piece
                else:
                    out_ref[r, pair * 2 + c] += piece
            return 0

        lax.fori_loop(0, ROUNDS * 2, body, 0)

    whiten(0)
    pl.semaphore_wait(barrier, 2 * PEERS + 6 - 2 * alone.astype(jnp.int32))
    send_in(0)
    whiten(1)
    send_in(1)
    for k in range(SUB):
        wait_in(k)
        regroup(k)
        send_ring(k)
        cross(k, 0, 0, back.at[k, 0], lambda f: pass_on(k, f))
        send_out(k, 0)
        cross(k, 0, 1, back.at[k, 1], lambda f: next_copy(k, f).wait_recv())
        for f in range(FSUB):
            third_copy(k, f).wait_recv()
        cross(k, 1, 2, loan.at[k], lambda f: None)
        loan_copy(k).start()
        cross(k, 0, 2, back.at[k, 2], lambda f: None)
        loan_copy(k).wait_recv()
        send_out(k, 1)
    for k in range(SUB):
        wait_out(k)
        to_lags(k)

    for k in range(SUB):
        end_ring(k)

        def finish(n, _):
            @pl.when(jnp.logical_not(jnp.logical_and(alone, n == chunk)))
            def _():
                in_copy(k, n, dev).wait_send()

            @pl.when(jnp.logical_not(jnp.logical_and(alone, n == dev)))
            def _():
                for late in range(2):
                    out_copy(k, late, n, chunk).wait_send()

            return 0

        lax.fori_loop(0, PEERS, finish, 0)


def local(spectra, validity):
    pieces = spectra.reshape(PARTS, PEERS, SUB, FSUB, OWN, WINDOWS).transpose(2, 1, 0, 4, 3, 5)
    pieces = pieces.reshape(SUB, PEERS, PARTS, ROWS, WINDOWS)
    mask = jnp.repeat(validity.astype(jnp.float32), FSUB, axis=0)
    table = jnp.asarray(lag_table())
    vmem = pl.BlockSpec(memory_space=pltpu.VMEM)
    dma = pltpu.SemaphoreType.DMA
    return pl.pallas_call(
        kernel,
        out_shape=jax.ShapeDtypeStruct((ROUNDS, OWN, GROUP, LAGS), jnp.float32),
        in_specs=[vmem, vmem, vmem],
        out_specs=vmem,
        scratch_shapes=[
            pltpu.VMEM((SUB, PEERS, PARTS, ROWS, WINDOWS), jnp.bfloat16),
            pltpu.VMEM((SUB, PEERS, PARTS, ROWS, WINDOWS), jnp.bfloat16),
            pltpu.VMEM((WINDOWS // LANES, PEERS * ROWS, LANES), jnp.float32),
            pltpu.VMEM((SUB, 3, FSUB, GROUP, PARTS * WINDOWS), jnp.bfloat16),
            pltpu.VMEM((SUB, FSUB, GROUP, PARTS * WINDOWS), jnp.bfloat16),
            pltpu.VMEM((2 * GROUP, PARTS * WINDOWS), jnp.bfloat16),
            pltpu.VMEM((GROUP * PARTS * FSUB, LANES), jnp.float32),
            pltpu.VMEM((SUB, PEERS, BACK_ROWS, LANES), jnp.bfloat16),
            pltpu.VMEM((SUB, ROUNDS, PEERS, BACK_ROWS, LANES), jnp.bfloat16),
            pltpu.VMEM((SUB, PEERS, ROUNDS, BACK_ROWS, LANES), jnp.bfloat16),
            dma((SUB, PEERS)), dma((SUB, PEERS)),
            dma((SUB, 4, FSUB)), dma((SUB, 4, FSUB)),
            dma((SUB, 2, PEERS)), dma((SUB, 2, PEERS)),
            dma((3 * SUB,)),
        ],
        compiler_params=pltpu.CompilerParams(
            collective_id=1, has_side_effects=True, vmem_limit_bytes=48 << 20),
        name="correlate",
    )(pieces, mask, table)


def solution(mesh):
    in_specs = (P(None, None, ("grp", "dev"), None), P(("grp", "dev"), None))
    out_specs = P(None, ("grp", "dev"), None, None)
    return jax.shard_map(local, mesh=mesh, in_specs=in_specs, out_specs=out_specs, check_vma=False)
```

time: 272 us -> 196 us (0.72)
  the two profiles are of different devices: /device:TPU:47 before, /device:TPU:57 now
where the time goes in v2:
time: 196 us; the launch traced here: 195 us
  Pallas kernels  188 us (96%)
  local copies, waits for them, and re-layouts  7.02 us (4%)
    pallas_call x1, Pallas kernels, local(): pl.pallas_call(kernel, out_shape=jax.ShapeDtypeStruct((ROUNDS, OWN, GROUP...  188 us

profile of v2, /device:TPU:57, one launch (start us, length us, event | category | flops | bytes accessed | tf_op | source)
XLA Modules:
  0.0 195.4 jit_solution(16620655199748936245)
XLA Ops:
  0.0 3.2 %copy.6 = bf16[2,32,2,4,4,384]{5,3,4,0,1,2:T(4,128)(2,1)} copy(bf16[2,32,2,4,4,384]{5,4,3,2,1,0:T(4,128)(2,1)} %bitcast.5) | data formatting | bytes 3145728 | tf_op jit(solution)/shard_map/reshape | solution.py:336
  3.2 0.0 copy-start.1
  3.2 0.0 copy-start
  3.2 2.8 %reshape.10.x_ref = bf16[2,32,2,16,384]{4,3,2,1,0:T(8,128)(2,1)S(1)} reshape(bf16[2,32,2,4,4,384]{5,4,3,2,1,0:T(4,128)(2,1)} %bitcast.4) | data formatting | bytes 3145728 | tf_op jit(solution)/shard_map/reshape | solution.py:337
  6.0 0.0 copy-done.1
  6.1 0.0 copy-done
  6.1 188.4 %correlate.1 = f32[4,4,128,128]{3,2,1,0:T(8,128)S(1)} custom-call(bf16[2,32,2,16,384]{4,3,2,1,0:T(8,128)(2,1)S(1)} %reshape.10.x_ref, f32[16,384]{1,0:T(8,128)S(1)} %reshape.11.mask_ref, bf16[2,512,512]{2,1,0:T(8,128)(2,1)S(1)} %copy-done), custom_call_target="tpu_custom_call" | custom-call | tf_op jit(solution)/shard_map/correlate/pallas_call | solution.py:342
  194.5 1.0 copy.8
  (3 shorter events, 0.0 us)
Async XLA Ops:
  3.2 2.8 %copy-start.1 = (s32[4,384]{1,0:T(4,128)S(1)}, s32[4,384]{1,0:T(4,128)}, u32[]{:S(2)}) copy-start(s32[4,384]{1,0:T(4,128)} %param.4) | copy-start | bytes 18436
  3.2 2.9 %copy-start = (bf16[2,512,512]{2,1,0:T(8,128)(2,1)S(1)}, bf16[2,512,512]{2,1,0:T(8,128)(2,1)}, u32[]{:S(2)}) copy-start(bf16[2,512,512]{2,1,0:T(8,128)(2,1)} %constant.2.clone.table_ref) | copy-start | bytes 3145732

commit v3 on v2

v3 whole, which is shorter than its diff:
```python
import jax
import jax.numpy as jnp
import numpy as np
from jax import lax
from jax.experimental import pallas as pl
from jax.experimental.pallas import tpu as pltpu
from jax.sharding import PartitionSpec as P

MESH = pl.DeviceIdType.MESH
FREQS = 256
LAGS = 128
ROUNDS = 4
WINDOWS = 384
GROUP = 128
PEERS = 32
PARTS = 2
SUB = 2
FSUB = FREQS // PEERS // SUB
OWN = GROUP // PEERS
ROWS = OWN * FSUB
BACK_ROWS = OWN * PARTS * FSUB
LANES = 128
PLANE_ROWS = 4 * PARTS * FSUB
BATCH = 4
PLANES = 16
REACH = 7
NEAR = 3
PLACES = 2 * REACH + NEAR
HOP = 2
BATCHES = (((0, 1), (1, 4)), ((0, 1), (1, 2), (2, 3), (3, 4)))


def lag_table():
    freq = np.arange(FREQS, dtype=np.int64)[:, None]
    lag = np.arange(LAGS, dtype=np.int64)[None, :] - LAGS // 2
    angle = np.pi * np.mod(freq * lag, 2 * FREQS) / FREQS
    signed = np.stack([np.cos(angle), -np.sin(angle)], axis=0).astype(np.float32)
    upper = signed.astype(jnp.bfloat16)
    lower = (signed - upper.astype(np.float32)).astype(jnp.bfloat16)
    split = np.stack([upper, lower], axis=0)
    split = split.reshape(2, PARTS, SUB, PEERS, FSUB, LAGS)
    split = split.transpose(2, 3, 1, 4, 0, 5)
    table = np.zeros((SUB, PEERS, 2, PARTS, FSUB, 2, 2, LAGS), dtype=jnp.bfloat16)
    for pair in range(2):
        table[:, :, pair, :, :, :, pair, :] = split
    table = table.reshape(SUB, PEERS * 2 * PARTS * FSUB, 4 * LAGS)
    return np.concatenate([table, table[:, :(REACH - 1) * PLANE_ROWS]], axis=1)


def kernel(x_hbm, valid_ref, table_hbm, out_ref, x_ref, table_ref, stage, send, recv, spread, blocks, carry, left, terms, loan, back, home, sums, part, got,
           send_sem, recv_sem, ring_send, ring_recv, back_send, back_recv, part_send, part_recv, self_sem, load_sem):
    grp = lax.axis_index("grp")
    dev = lax.axis_index("dev")
    z_lo, y = grp // 4, grp % 4
    x, z_hi, core = dev // 8, (dev // 2) % 4, dev % 2
    plane = z_hi * 4 + z_lo
    chunk = plane * 2 + core
    flip = 1 - 2 * (z_lo % 2)
    held = (z_lo + flip * x + 4) % 4
    alone = x == 0

    def worker(q):
        at = q // 2
        column = ((z_lo - at) * (1 - 2 * (at % 2)) + 32) % 4
        return (at % 4 * 4 + y, column * 8 + at // 4 * 2 + q % 2)

    def owner(s):
        return (held * 4 + y, s)

    def at_plane(at):
        return (at % 4 * 4 + y, x * 8 + at // 4 * 2 + core)

    def load_x(k):
        half = pl.ds(k * FREQS // SUB, FREQS // SUB)
        return pltpu.make_async_copy(x_hbm.at[:, half], x_ref.at[:, half], load_sem.at[k])

    load_table = pltpu.make_async_copy(table_hbm, table_ref, load_sem.at[SUB])
    for k in range(SUB):
        load_x(k).start()
    load_table.start()

    def route(n):
        s = (x + n // 4) % 4 * 8 + (z_hi + 2 + n) % 4 * 2 + (core + n // 16) % 2
        goal = s // 2 % 4 * 4 + held
        away = (plane - goal + 7 + PLANES) % PLANES - 7
        away = away - PLANES * jnp.logical_and(away == 8, held % 2 == 1).astype(jnp.int32)
        after, before = (away >= HOP).astype(jnp.int32), (away <= -HOP).astype(jnp.int32)
        place = away + 15 - after * 17
        stop = (goal + HOP * (after - before) + PLANES) % PLANES
        here = jnp.logical_and(stop == plane, jnp.logical_and(s // 8 == x, s % 2 == core))
        return s, place, (stop % 4 * 4 + y, s // 8 * 8 + stop // 4 * 2 + s % 2), here

    def origin(place, c):
        if place < REACH:
            goal, at = plane - HOP, plane + place
        elif place < 2 * REACH:
            goal, at = plane + HOP, plane + place - 13
        else:
            goal, at = plane, plane + place - 15
        at = (at + PLANES) % PLANES
        column = (((goal + PLANES) % 4 - at) * (1 - 2 * (at % 2)) + 32) % 4
        here = jnp.logical_and(at == plane, jnp.logical_and(column == x, c == core))
        return (at % 4 * 4 + y, column * 8 + at // 4 * 2 + c), here

    odd = z_lo % 2
    unused = lax.select(odd == 1, jnp.int32(REACH - 1), jnp.int32(REACH))

    def ring(by):
        g = (held * 4 + y + by + 16) % 16
        column = ((g // 4 - z_lo) * flip + 8) % 4
        return (z_lo * 4 + g % 4, column * 8 + z_hi * 2 + core)

    barrier = pltpu.get_barrier_semaphore()

    for i in range(PEERS):
        @pl.when(jnp.logical_not(jnp.logical_and(alone, i == dev)))
        def _():
            pl.semaphore_signal(barrier, inc=1, device_id=owner(i), device_id_type=MESH)


    for place in range(PLACES):
        for c in range(2):
            source, here = origin(place, c)
            far = jnp.logical_not(here)
            if place in (REACH - 1, REACH):
                far = jnp.logical_and(far, place != unused)

            @pl.when(far)
            def _():
                pl.semaphore_signal(barrier, inc=1, device_id=source, device_id_type=MESH)

    for by in (HOP, -HOP):
        pl.semaphore_signal(barrier, inc=1, device_id=at_plane((plane + by + PLANES) % PLANES), device_id_type=MESH)
    for by in (-1, -3, 3, -4, 1):
        pl.semaphore_signal(barrier, inc=1, device_id=ring(by), device_id_type=MESH)

    def in_copy(k, q, s):
        return pltpu.make_async_remote_copy(
            src_ref=send.at[k, q], dst_ref=recv.at[k, s], send_sem=send_sem.at[k, q],
            recv_sem=recv_sem.at[k, s], device_id=worker(q), device_id_type=MESH)

    def in_self(k):
        return pltpu.make_async_copy(send.at[k, chunk], recv.at[k, dev], self_sem.at[k])

    def nth(n):
        step = n // 2
        off = lax.select(step % 2 == 0, 8 - step // 2, step // 2 - 7)
        return (plane + off + 16) % 16 * 2 + (core + n) % 2

    def put(k, q):
        here = jnp.logical_and(alone, q == chunk)

        @pl.when(jnp.logical_not(here))
        def _():
            in_copy(k, q, dev).start()

        @pl.when(here)
        def _():
            in_self(k).start()

    def send_in(k):
        def body(n, _):
            for b in range(BATCH):
                q = nth(n * BATCH + b)
                at = (k * PEERS + q) * FSUB
                masked = x_ref[:, pl.ds(at, FSUB)].astype(jnp.float32) * valid_ref[...].astype(jnp.float32)[None, None]
                power = jnp.sum(jnp.sum(masked * masked, axis=0, keepdims=True), axis=3, keepdims=True) / WINDOWS + 1e-06
                whitened = masked / jnp.sqrt(power)
                for part in range(PARTS):
                    for w in range(WINDOWS // LANES):
                        for f in range(FSUB):
                            stage[b, part, w, pl.ds(f, OWN, stride=FSUB), :] = whitened[
                                part, f, :, w * LANES:(w + 1) * LANES]
            for b in range(BATCH):
                for part in range(PARTS):
                    for w in range(WINDOWS // LANES):
                        send[k, nth(n * BATCH + b), part, :, w * LANES:(w + 1) * LANES] = stage[b, part, w].astype(jnp.bfloat16)
            for b in range(BATCH):
                put(k, nth(n * BATCH + b))
            return 0

        lax.fori_loop(0, PEERS // BATCH, body, 0)

    def wait_in(k):
        def body(s, _):
            here = jnp.logical_and(alone, s == dev)

            @pl.when(jnp.logical_not(here))
            def _():
                in_copy(k, s, s).wait_recv()

            @pl.when(here)
            def _():
                in_self(k).wait()

            return 0

        lax.fori_loop(0, PEERS, body, 0)

    def regroup(k):
        for part in range(PARTS):
            for w in range(WINDOWS // LANES):
                spread[w] = recv[k, :, part, :, w * LANES:(w + 1) * LANES].astype(jnp.float32).reshape(
                    PEERS * ROWS, LANES)
            for f in range(FSUB):
                for w in range(WINDOWS // LANES):
                    at = part * WINDOWS + w * LANES
                    blocks[k, 0, f, :, at:at + LANES] = spread[
                        w, pl.ds(f, GROUP, stride=FSUB), :].astype(jnp.bfloat16)

    def ring_copy(by, src, dst, k, which, f):
        return pltpu.make_async_remote_copy(
            src_ref=src, dst_ref=dst, send_sem=ring_send.at[k, which, f], recv_sem=ring_recv.at[k, which, f],
            device_id=ring(by), device_id_type=MESH)

    def next_copy(k, f):
        return ring_copy(1, blocks.at[k, 0, f], blocks.at[k, 1, f], k, 0, f)

    def third_copy(k, f):
        return ring_copy(3, blocks.at[k, 0, f], blocks.at[k, 2, f], k, 1, f)

    def turn_copy(k, f):
        return ring_copy(-3, blocks.at[k, 0, f], carry.at[k, f], k, 2, f)

    def pass_copy(k, f):
        return ring_copy(4, carry.at[k, f], blocks.at[k, 1, f], k, 0, f)

    def loan_copy(k):
        return ring_copy(-1, loan.at[k], back.at[k, 3], k, 3, 0)

    def send_ring(k):
        next_copy(k, FSUB - 1).start()
        for f in range(FSUB):
            if f < FSUB - 1:
                @pl.when(y < 3)
                def _():
                    next_copy(k, f).start()

                @pl.when(y == 3)
                def _():
                    turn_copy(k, f).start()

            third_copy(k, f).start()

    def pass_on(k, f):
        @pl.when(jnp.logical_and(y == 0, f < FSUB - 1))
        def _():
            turn_copy(k, f).wait_recv()
            pass_copy(k, f).start()

    def end_ring(k):
        next_copy(k, FSUB - 1).wait_send()
        for f in range(FSUB):
            if f < FSUB - 1:
                @pl.when(y < 3)
                def _():
                    next_copy(k, f).wait_send()

                @pl.when(y == 3)
                def _():
                    turn_copy(k, f).wait_send()

                @pl.when(y == 0)
                def _():
                    pass_copy(k, f).wait_send()

            third_copy(k, f).wait_send()
        loan_copy(k).wait_send()

    def cross(k, one, other, put, ready):
        def body(f, _):
            ready(f)
            own = blocks[k, one, f]
            left[0:GROUP, :] = own
            left[GROUP:, 0:WINDOWS] = own[:, WINDOWS:]
            left[GROUP:, WINDOWS:] = -own[:, :WINDOWS]
            product = lax.dot_general(
                left[...], blocks[k, other, f], (((1,), (1,)), ((), ())), preferred_element_type=jnp.float32)
            for part in range(PARTS):
                terms[pl.ds(part * FSUB + f, GROUP, stride=PARTS * FSUB), :] = product[
                    part * GROUP:(part + 1) * GROUP]
            return 0

        lax.fori_loop(0, FSUB, body, 0)
        put[...] = terms[...].astype(jnp.bfloat16).reshape(PEERS, BACK_ROWS, LANES)

    def out_refs(k, late, s, place, c):
        first, last = BATCHES[k][late]
        return back.at[k, first:last, s], home.at[k, place, c, first:last]

    def out_copy(k, late, n):
        s, place, target, here = route(n)
        src, dst = out_refs(k, late, s, place, core)
        far = pltpu.make_async_remote_copy(
            src_ref=src, dst_ref=dst, send_sem=back_send.at[k, late, n],
            recv_sem=back_recv.at[k, late, place, core], device_id=target, device_id_type=MESH)
        return here, far, pltpu.make_async_copy(src, dst, back_recv.at[k, late, place, core])

    def send_out(k, late):
        def body(n, _):
            here, far, near = out_copy(k, late, n)

            @pl.when(jnp.logical_not(here))
            def _():
                far.start()

            @pl.when(here)
            def _():
                near.start()

            return 0

        lax.fori_loop(0, PEERS, body, 0)

    def wait_out(k, late, lowest, highest):
        def body(n, _):
            place, c = n // 2, n % 2

            @pl.when(place != unused)
            def _():
                _, dst = out_refs(k, late, 0, place, c)
                pltpu.make_async_copy(dst, dst, back_recv.at[k, late, place, c]).wait()

            return 0

        lax.fori_loop(2 * lowest, 2 * highest, body, 0)

    scale = 1.0 / np.sqrt(np.float32(WINDOWS) * FREQS)

    def lags(k, lowest, count, start, slot, pair):
        rows = pl.multiple_of(pair * 16, 16)
        values = home[k, lowest:lowest + count, :, slot, pl.ds(rows, 16), :].reshape(count * PLANE_ROWS, LANES)
        window = pl.ds(pl.multiple_of((start + PLANES) % PLANES * PLANE_ROWS, PLANE_ROWS), count * PLANE_ROWS)
        both = lax.dot_general(
            values, table_ref[k, window, :], (((0,), (0,)), ((), ())), preferred_element_type=jnp.float32)
        return (both[:, :2 * LAGS] + both[:, 2 * LAGS:]) * scale

    def reach_lags(k, side, slot, pair):
        return lags(k, side * REACH, REACH, plane - side * (REACH - 1), slot, pair)

    def gather_first():
        def body(n, _):
            slot, pair = n // 2, n % 2
            for side in range(2):
                values = reach_lags(0, side, slot, pair)
                for c in range(2):
                    sums[side, slot, pair * 2 + c] = values[:, c * LAGS:(c + 1) * LAGS]
            return 0

        lax.fori_loop(0, ROUNDS * 2, body, 0)

    def part_copy(side, slot):
        goal = (plane + (2 * side - 1) * HOP + PLANES) % PLANES
        return pltpu.make_async_remote_copy(
            src_ref=part.at[side, slot], dst_ref=got.at[side, slot], send_sem=part_send.at[side, slot],
            recv_sem=part_recv.at[side, slot], device_id=at_plane(goal), device_id_type=MESH)

    def gather_last(slot):
        def body(pair, _):
            for side in range(2):
                values = reach_lags(1, side, slot, pair)
                for c in range(2):
                    total = sums[side, slot, pair * 2 + c] + values[:, c * LAGS:(c + 1) * LAGS]
                    part[side, slot, pair * 2 + c] = total.astype(jnp.bfloat16)
            return 0

        lax.fori_loop(0, 2, body, 0)
        for side in range(2):
            part_copy(side, slot).start()

    def round_of(slot):
        return slot + (slot == 2).astype(jnp.int32) - (slot == 3).astype(jnp.int32)

    def near_lags():
        def body(n, _):
            slot, pair = n // 2, n % 2
            values = lags(0, 2 * REACH, NEAR, plane - 1, slot, pair) + lags(1, 2 * REACH, NEAR, plane - 1, slot, pair)
            for c in range(2):
                out_ref[round_of(slot), pair * 2 + c] = values[:, c * LAGS:(c + 1) * LAGS]
            return 0

        lax.fori_loop(0, ROUNDS * 2, body, 0)

    def add_parts(slot):
        def body(c, _):
            r = (0, 1, 3, 2)[slot]
            out_ref[r, c] += got[0, slot, c].astype(jnp.float32) + got[1, slot, c].astype(jnp.float32)
            return 0

        lax.fori_loop(0, OWN, body, 0)

    for k in range(SUB):
        home[k, unused] = jnp.zeros((2, ROUNDS, BACK_ROWS, LANES), jnp.bfloat16)
    load_x(0).wait()
    targets = 2 * PEERS + 7 - 2 * (x == 0).astype(jnp.int32) - 2 * (x == 2).astype(jnp.int32)
    pl.semaphore_wait(barrier, targets)
    send_in(0)
    load_x(1).wait()
    send_in(1)
    for k in range(SUB):
        wait_in(k)
        regroup(k)
        send_ring(k)
        cross(k, 0, 0, back.at[k, 0], lambda f: pass_on(k, f))
        send_out(k, 0)
        cross(k, 0, 1, back.at[k, 1], lambda f: next_copy(k, f).wait_recv())
        if k > 0:
            send_out(k, 1)
        for f in range(FSUB):
            third_copy(k, f).wait_recv()
        cross(k, 1, 2, loan.at[k], lambda f: None)
        loan_copy(k).start()
        cross(k, 0, 2, back.at[k, 2], lambda f: None)
        if k > 0:
            send_out(k, 2)
        loan_copy(k).wait_recv()
        send_out(k, len(BATCHES[k]) - 1)
    load_table.wait()
    wait_out(0, 0, 0, 2 * REACH)
    wait_out(0, 1, 0, 2 * REACH)
    gather_first()
    for slot in range(ROUNDS):
        wait_out(1, slot, 0, 2 * REACH)
        gather_last(slot)
    for k in range(SUB):
        for late in range(len(BATCHES[k])):
            wait_out(k, late, 2 * REACH, PLACES)
    near_lags()
    for slot in range(ROUNDS):
        for side in range(2):
            part_copy(side, slot).wait_recv()
        add_parts(slot)
    for slot in range(ROUNDS):
        for side in range(2):
            part_copy(side, slot).wait_send()
    for k in range(SUB):
        end_ring(k)

        def finish(n, _):
            @pl.when(jnp.logical_not(jnp.logical_and(alone, n == chunk)))
            def _():
                in_copy(k, n, dev).wait_send()

            for late in range(len(BATCHES[k])):
                here, far, _ = out_copy(k, late, n)

                @pl.when(jnp.logical_not(here))
                def _():
                    far.wait_send()

            return 0

        lax.fori_loop(0, PEERS, finish, 0)


def local(spectra, validity):
    table = jnp.asarray(lag_table())
    vmem = pl.BlockSpec(memory_space=pltpu.VMEM)
    anywhere = pl.BlockSpec(memory_space=pl.ANY)
    dma = pltpu.SemaphoreType.DMA
    return pl.pallas_call(
        kernel,
        out_shape=jax.ShapeDtypeStruct((ROUNDS, OWN, GROUP, LAGS), jnp.float32),
        in_specs=[anywhere, vmem, anywhere],
        out_specs=vmem,
        scratch_shapes=[
            pltpu.VMEM((PARTS, FREQS, OWN, WINDOWS), jnp.bfloat16),
            pltpu.VMEM((SUB, (PLANES + REACH - 1) * PLANE_ROWS, 4 * LANES), jnp.bfloat16),
            pltpu.VMEM((BATCH, PARTS, WINDOWS // LANES, ROWS, LANES), jnp.float32),
            pltpu.VMEM((SUB, PEERS, PARTS, ROWS, WINDOWS), jnp.bfloat16),
            pltpu.VMEM((SUB, PEERS, PARTS, ROWS, WINDOWS), jnp.bfloat16),
            pltpu.VMEM((WINDOWS // LANES, PEERS * ROWS, LANES), jnp.float32),
            pltpu.VMEM((SUB, 3, FSUB, GROUP, PARTS * WINDOWS), jnp.bfloat16),
            pltpu.VMEM((SUB, FSUB, GROUP, PARTS * WINDOWS), jnp.bfloat16),
            pltpu.VMEM((2 * GROUP, PARTS * WINDOWS), jnp.bfloat16),
            pltpu.VMEM((GROUP * PARTS * FSUB, LANES), jnp.float32),
            pltpu.VMEM((SUB, PEERS, BACK_ROWS, LANES), jnp.bfloat16),
            pltpu.VMEM((SUB, ROUNDS, PEERS, BACK_ROWS, LANES), jnp.bfloat16),
            pltpu.VMEM((SUB, PLACES, 2, ROUNDS, BACK_ROWS, LANES), jnp.bfloat16),
            pltpu.VMEM((2, ROUNDS, OWN, GROUP, LAGS), jnp.float32),
            pltpu.VMEM((2, ROUNDS, OWN, GROUP, LAGS), jnp.bfloat16),
            pltpu.VMEM((2, ROUNDS, OWN, GROUP, LAGS), jnp.bfloat16),
            dma((SUB, PEERS)), dma((SUB, PEERS)),
            dma((SUB, 4, FSUB)), dma((SUB, 4, FSUB)),
            dma((SUB, ROUNDS, PEERS)), dma((SUB, ROUNDS, PLACES, 2)),
            dma((2, ROUNDS)), dma((2, ROUNDS)),
            dma((SUB,)), dma((SUB + 1,)),
        ],
        compiler_params=pltpu.CompilerParams(
            collective_id=1, has_side_effects=True, vmem_limit_bytes=56 << 20),
        name="correlate",
    )(spectra, validity, table)


def solution(mesh):
    in_specs = (P(None, None, ("grp", "dev"), None), P(("grp", "dev"), None))
    out_specs = P(None, ("grp", "dev"), None, None)
    return jax.shard_map(local, mesh=mesh, in_specs=in_specs, out_specs=out_specs, check_vma=False)
```

time: 196 us -> 189 us (0.964)
  the two profiles are of different devices: /device:TPU:57 before, /device:TPU:48 now
where the time goes in v3:
time: 189 us
  Pallas kernels  187 us (99%)
  local copies, waits for them, and re-layouts  2.3 us (1%)
    pallas_call x1, Pallas kernels, local(): pl.pallas_call(kernel, out_shape=jax.ShapeDtypeStruct((ROUNDS, OWN, GROUP...  187 us

profile of v3, /device:TPU:48, one launch (start us, length us, event | category | flops | bytes accessed | tf_op | source)
XLA Modules:
  0.0 188.9 jit_solution(14390158316206898069)
XLA Ops:
  0.0 186.6 %correlate.1 = f32[4,4,128,128]{3,2,1,0:T(8,128)} custom-call(bf16[2,256,4,384]{3,2,1,0:T(4,128)(2,1)} %x_hbm.1, s32[4,384]{1,0:T(4,128)} %valid_ref.1, bf16[2,704,512]{2,1,0:T(8,128)(2,1)} %constant.2.clone.table_hbm), custom_call_target="tpu_custom_call" | custom-call | tf_op jit(solution)/shard_map/correlate/pallas_call | solution.py:461
  186.6 2.3 %copy.5 = f32[4,4,128,128]{3,2,1,0:T(8,128)} copy(f32[4,4,128,128]{3,2,1,0:T(8,128)} %correlate.1) | data formatting | bytes 2097152

commit v4 on v3

--- a/solution.py
+++ b/solution.py
@@ -369,28 +369,46 @@
             part_copy(side, slot).start()
 
     def round_of(slot):
-        return slot + (slot == 2).astype(jnp.int32) - (slot == 3).astype(jnp.int32)
-
-    def near_lags():
-        def body(n, _):
-            slot, pair = n // 2, n % 2
+        return (0, 1, 3, 2)[slot]
+
+    def near_lags(slot):
+        def body(pair, _):
             values = lags(0, 2 * REACH, NEAR, plane - 1, slot, pair) + lags(1, 2 * REACH, NEAR, plane - 1, slot, pair)
             for c in range(2):
                 out_ref[round_of(slot), pair * 2 + c] = values[:, c * LAGS:(c + 1) * LAGS]
             return 0
 
-        lax.fori_loop(0, ROUNDS * 2, body, 0)
+        lax.fori_loop(0, 2, body, 0)
 
     def add_parts(slot):
         def body(c, _):
-            r = (0, 1, 3, 2)[slot]
-            out_ref[r, c] += got[0, slot, c].astype(jnp.float32) + got[1, slot, c].astype(jnp.float32)
+            out_ref[round_of(slot), c] += got[0, slot, c].astype(jnp.float32) + got[1, slot, c].astype(jnp.float32)
             return 0
 
         lax.fori_loop(0, OWN, body, 0)
 
-    for k in range(SUB):
-        home[k, unused] = jnp.zeros((2, ROUNDS, BACK_ROWS, LANES), jnp.bfloat16)
+    def end_in(k):
+        def body(n, _):
+            @pl.when(jnp.logical_not(jnp.logical_and(alone, n == chunk)))
+            def _():
+                in_copy(k, n, dev).wait_send()
+
+            return 0
+
+        lax.fori_loop(0, PEERS, body, 0)
+
+    def end_out(k, late):
+        def body(n, _):
+            here, far, _ = out_copy(k, late, n)
+
+            @pl.when(jnp.logical_not(here))
+            def _():
+                far.wait_send()
+
+            return 0
+
+        lax.fori_loop(0, PEERS, body, 0)
+
     load_x(0).wait()
     targets = 2 * PEERS + 7 - 2 * (x == 0).astype(jnp.int32) - 2 * (x == 2).astype(jnp.int32)
     pl.semaphore_wait(barrier, targets)
@@ -403,6 +421,7 @@
         send_ring(k)
         cross(k, 0, 0, back.at[k, 0], lambda f: pass_on(k, f))
         send_out(k, 0)
+        end_in(k)
         cross(k, 0, 1, back.at[k, 1], lambda f: next_copy(k, f).wait_recv())
         if k > 0:
             send_out(k, 1)
@@ -416,16 +435,22 @@
         loan_copy(k).wait_recv()
         send_out(k, len(BATCHES[k]) - 1)
     load_table.wait()
+    for k in range(SUB):
+        home[k, unused] = jnp.zeros((2, ROUNDS, BACK_ROWS, LANES), jnp.bfloat16)
     wait_out(0, 0, 0, 2 * REACH)
     wait_out(0, 1, 0, 2 * REACH)
     gather_first()
+    for late in range(len(BATCHES[0])):
+        wait_out(0, late, 2 * REACH, PLACES)
+        end_out(0, late)
+    end_ring(0)
     for slot in range(ROUNDS):
         wait_out(1, slot, 0, 2 * REACH)
         gather_last(slot)
-    for k in range(SUB):
-        for late in range(len(BATCHES[k])):
-            wait_out(k, late, 2 * REACH, PLACES)
-    near_lags()
+        wait_out(1, slot, 2 * REACH, PLACES)
+        near_lags(slot)
+        end_out(1, slot)
+    end_ring(1)
     for slot in range(ROUNDS):
         for side in range(2):
             part_copy(side, slot).wait_recv()
@@ -433,35 +458,17 @@
     for slot in range(ROUNDS):
         for side in range(2):
             part_copy(side, slot).wait_send()
-    for k in range(SUB):
-        end_ring(k)
-
-        def finish(n, _):
-            @pl.when(jnp.logical_not(jnp.logical_and(alone, n == chunk)))
-            def _():
-                in_copy(k, n, dev).wait_send()
-
-            for late in range(len(BATCHES[k])):
-                here, far, _ = out_copy(k, late, n)
-
-                @pl.when(jnp.logical_not(here))
-                def _():
-                    far.wait_send()
-
-            return 0
-
-        lax.fori_loop(0, PEERS, finish, 0)
 
 
 def local(spectra, validity):
     table = jnp.asarray(lag_table())
     vmem = pl.BlockSpec(memory_space=pltpu.VMEM)
-    anywhere = pl.BlockSpec(memory_space=pl.ANY)
+    main = pl.BlockSpec(memory_space=pltpu.HBM)
     dma = pltpu.SemaphoreType.DMA
     return pl.pallas_call(
         kernel,
         out_shape=jax.ShapeDtypeStruct((ROUNDS, OWN, GROUP, LAGS), jnp.float32),
-        in_specs=[anywhere, vmem, anywhere],
+        in_specs=[main, vmem, main],
         out_specs=vmem,
         scratch_shapes=[
             pltpu.VMEM((PARTS, FREQS, OWN, WINDOWS), jnp.bfloat16),
@@ -487,7 +494,7 @@
             dma((SUB,)), dma((SUB + 1,)),
         ],
         compiler_params=pltpu.CompilerParams(
-            collective_id=1, has_side_effects=True, vmem_limit_bytes=56 << 20),
+            collective_id=1, has_side_effects=True, vmem_limit_bytes=54 << 20),
         name="correlate",
     )(spectra, validity, table)
 

time: 189 us -> 186 us (0.984)
  the two profiles are of different devices: /device:TPU:48 before, /device:TPU:40 now
where the time goes in v4:
time: 186 us
  Pallas kernels  184 us (99%)
  local copies, waits for them, and re-layouts  2.3 us (1%)
    pallas_call x1, Pallas kernels, local(): pl.pallas_call(kernel, out_shape=jax.ShapeDtypeStruct((ROUNDS, OWN, GROUP...  184 us

profile of v4, /device:TPU:40, one launch (start us, length us, event | category | flops | bytes accessed | tf_op | source)
XLA Modules:
  0.0 185.9 jit_solution(9817399965493585617)
XLA Ops:
  0.0 183.6 %correlate.1 = f32[4,4,128,128]{3,2,1,0:T(8,128)} custom-call(bf16[2,256,4,384]{3,2,1,0:T(4,128)(2,1)} %x_hbm.1, s32[4,384]{1,0:T(4,128)} %valid_ref.1, bf16[2,704,512]{2,1,0:T(8,128)(2,1)} %constant.2.clone.table_hbm), custom_call_target="tpu_custom_call" | custom-call | tf_op jit(solution)/shard_map/correlate/pallas_call | solution.py:468
  183.6 2.3 %copy.5 = f32[4,4,128,128]{3,2,1,0:T(8,128)} copy(f32[4,4,128,128]{3,2,1,0:T(8,128)} %correlate.1) | data formatting | bytes 2097152

commit v5 on v4

--- a/solution.py
+++ b/solution.py
@@ -27,7 +27,7 @@
 NEAR = 3
 PLACES = 2 * REACH + NEAR
 HOP = 2
-BATCHES = (((0, 1), (1, 4)), ((0, 1), (1, 2), (2, 3), (3, 4)))
+BATCHES = (((0, 4),), ((0, 1), (1, 2), (2, 3), (3, 4)))
 
 
 def lag_table():
@@ -420,7 +420,8 @@
         regroup(k)
         send_ring(k)
         cross(k, 0, 0, back.at[k, 0], lambda f: pass_on(k, f))
-        send_out(k, 0)
+        if k > 0:
+            send_out(k, 0)
         end_in(k)
         cross(k, 0, 1, back.at[k, 1], lambda f: next_copy(k, f).wait_recv())
         if k > 0:
@@ -438,7 +439,6 @@
     for k in range(SUB):
         home[k, unused] = jnp.zeros((2, ROUNDS, BACK_ROWS, LANES), jnp.bfloat16)
     wait_out(0, 0, 0, 2 * REACH)
-    wait_out(0, 1, 0, 2 * REACH)
     gather_first()
     for late in range(len(BATCHES[0])):
         wait_out(0, late, 2 * REACH, PLACES)

time: 186 us -> 186 us (level)
  the two profiles are of different devices: /device:TPU:40 before, /device:TPU:27 now
where the time goes in v5:
time: 186 us
  Pallas kernels  184 us (99%)
  local copies, waits for them, and re-layouts  2.3 us (1%)
    pallas_call x1, Pallas kernels, local(): pl.pallas_call(kernel, out_shape=jax.ShapeDtypeStruct((ROUNDS, OWN, GROUP...  184 us

profile of v5, /device:TPU:27, one launch (start us, length us, event | category | flops | bytes accessed | tf_op | source)
XLA Modules:
  0.0 186.3 jit_solution(10931662833898236923)
XLA Ops:
  0.0 184.0 %correlate.1 = f32[4,4,128,128]{3,2,1,0:T(8,128)} custom-call(bf16[2,256,4,384]{3,2,1,0:T(4,128)(2,1)} %x_hbm.1, s32[4,384]{1,0:T(4,128)} %valid_ref.1, bf16[2,704,512]{2,1,0:T(8,128)(2,1)} %constant.2.clone.table_hbm), custom_call_target="tpu_custom_call" | custom-call | tf_op jit(solution)/shard_map/correlate/pallas_call | solution.py:468
  184.0 2.3 %copy.5 = f32[4,4,128,128]{3,2,1,0:T(8,128)} copy(f32[4,4,128,128]{3,2,1,0:T(8,128)} %correlate.1) | data formatting | bytes 2097152
